TPU v7x, 512 devices: a whole 4x4x16 slice. The times are simulated.
512 devices in a mesh: wide: 128 (over y, z, x_hi), narrow: 4 (over x_lo, core).
Axes of the slice: x: 4 (x_hi: 2, x_lo: 2; x = x_hi * 2 + x_lo), y: 4, z: 16, core: 2. Of those that a mesh axis runs over, the one named last changes fastest.
Arguments:
- cells: bfloat16 [524288, 512], P(('wide', 'narrow')), may hold values from -700 to 700
- plate_id: int32 [524288], P(('wide', 'narrow')), may hold values from 0 to 127, as said below
- control: int32 [524288], P(('wide', 'narrow')), may hold values from 0 to 1, as said below
Outputs:
- sphered: bfloat16 [524288, 512], P(('wide', 'narrow'))
Inputs may be any that keep to these rules, and one draw needn't show every extreme that they name: `plate_id`: ids never fall; plate p begins at row p * 4096 + r_p with r_0 = 0 and 1024 <= r_p < 3072 for p >= 1, both ends reached by some plate. `control`: each aligned block of 1024 rows (the rows of one device) holds exactly 93 controls.
All inputs are finite; a program needn't handle non-finite values.
Results may differ from a plain program's by a relative error of at most 0.0071.
Values may be sent and summed in bfloat16 or wider, within the bound.
No kernel may reach another device: no remote copies, remote signals or barrier semaphores. Data moves between devices by JAX's collectives and lax.ppermute only.
A program may use at most 64 MiB of HBM per device.

v0:
```python
import jax
import jax.numpy as jnp
from jax import lax
from jax.sharding import PartitionSpec as P

ITERS = 4


shrink = 0.1
epsilon = 1e-05


def from_behind(value, axis, steps):
    count = lax.axis_size(axis)
    first, last = (max(0, -steps), min(count, count - steps))
    return lax.ppermute(value, axis, [(source, source + steps) for source in range(first, last)])


def highest_dot(left, right):
    return jnp.dot(left, right, precision=lax.Precision.HIGHEST)


def shards(cells, plate_id, control):
    rows_here, features = cells.shape
    members = lax.axis_size("narrow")
    quarter = features // members
    group_index = lax.axis_index("wide")
    member = lax.axis_index("narrow")
    row_offset = member * quarter
    slot_ids = group_index - 1 + jnp.arange(2, dtype=jnp.int32)
    chosen = (plate_id[:, None] == slot_ids[None, :]) & (control[:, None] == 1)
    chosen_weight = chosen.astype(jnp.bfloat16)
    picked = jnp.where(chosen[:, :, None], cells[:, None, :], jnp.zeros((), jnp.bfloat16)).reshape(
        rows_here, 2 * features
    )
    gram_blocks = jnp.einsum(
        "rk,rf->kf", picked, cells, preferred_element_type=jnp.float32
    ).reshape(2, features, features)
    column_sums = jnp.einsum("rk,rf->kf", chosen_weight, cells, preferred_element_type=jnp.float32)
    counts = jnp.sum(chosen.astype(jnp.float32), axis=0)
    gram_parts = lax.psum_scatter(gram_blocks, "narrow", scatter_dimension=1, tiled=True)
    sums_total, counts_total = lax.psum((column_sums, counts), "narrow")
    counts_row = jnp.broadcast_to(counts_total[:, None], (2, features))
    packed = jnp.concatenate([gram_parts, sums_total[:, None, :], counts_row[:, None, :]], axis=1)
    arrived = from_behind(packed[0], "wide", -1)
    combined = packed[1] + arrived
    gram_rows = combined[:quarter]
    column_total = combined[quarter]
    count_total = combined[quarter + 1, 0]
    centre = column_total / count_total
    centre_rows = lax.dynamic_slice_in_dim(centre, row_offset, quarter, 0)
    covariance_rows = gram_rows / count_total - centre_rows[:, None] * centre[None, :]
    covariance = lax.all_gather(covariance_rows, "narrow", axis=0, tiled=True)
    identity = jnp.eye(features, dtype=jnp.float32)
    trace_sum = jnp.sum(jnp.diagonal(covariance))
    shrunk = (1.0 - shrink) * covariance + (shrink * trace_sum / features + epsilon) * identity
    norm_scale = jnp.sqrt(jnp.sum(shrunk * shrunk))
    iterate = shrunk / norm_scale
    inverse = identity
    for iteration in range(ITERS):
        newton_step = 1.5 * identity - 0.5 * highest_dot(inverse, iterate)
        iterate = highest_dot(newton_step, iterate)
        inverse = highest_dot(newton_step, inverse)
    sphere_full = (inverse / jnp.sqrt(norm_scale)).astype(jnp.bfloat16)
    centre_half = centre.astype(jnp.bfloat16)
    whole = jnp.concatenate([sphere_full, centre_half[None, :]], axis=0)
    earlier = from_behind(whole, "wide", 1)
    spheres = jnp.stack([earlier[:features], sphere_full])
    centres = jnp.stack([earlier[features], centre_half])
    offsets = jnp.einsum("kf,kfg->kg", centres, spheres, preferred_element_type=jnp.float32)
    products = jnp.einsum("rf,kfg->rkg", cells, spheres, preferred_element_type=jnp.float32)
    own_rows = plate_id == group_index
    result = jnp.where(
        own_rows[:, None],
        products[:, 1, :] - offsets[1][None, :],
        products[:, 0, :] - offsets[0][None, :],
    )
    return result.astype(jnp.bfloat16)


def solution(mesh):
    return jax.shard_map(
        shards,
        mesh=mesh,
        in_specs=(P(("wide", "narrow"), None), P(("wide", "narrow")), P(("wide", "narrow"))),
        out_specs=P(("wide", "narrow"), None),
        check_vma=False,
    )
```

profile of v0, /device:TPU:25, one launch (start us, length us, event | category | flops | bytes accessed | tf_op | source)
XLA Modules:
  0.0 159.9 jit_solution(5455584733001376702)
XLA Ops:
  7.3 1.5 copy.7
  9.0 2.6 %fusion.4 = f32[2,512,512]{2,1,0:T(8,128)} fusion(pred[1024,2]{0,1:T(4,128)(4,1)S(1)} %get-tuple-element.10, bf16[1024,512]{1,0:T(8,128)(2,1)S(1)} %copy-done.1, bf16[1024,512]{0,1:T(8,128)(2,1)S(1)} %copy.7), kind=kOutput, calls=%fused_computation.8 | convolution fusion | flops 1074790400 | bytes 4196352 | tf_op jit(solution)/shard_map/rk,rf->kf/dot_general | solution.py:36
  11.9 5.8 %all-reduce = (f32[2]{0:T(128)S(1)}, f32[2,1,512]{2,1,0:T(1,128)S(1)}) all-reduce(f32[2]{0:T(128)S(1)} %get-tuple-element.9, f32[2,1,512]{2,1,0:T(1,128)S(1)} %broadcast_in_dim.49), channel_id=1, replica_groups=mesh['wide'=128,'narrow'=4] {'narrow'}, use_global_device_ids=true, to_apply=%region_3.4 | all-reduce | flops 1026 | bytes 8208 | tf_op jit(solution)/shard_map/psum | solution.py:42
  17.7 34.4 %reduce-scatter.2.cloned.1.call-done = f32[2,128,512]{2,1,0:T(8,128)} async-done(((f32[2,512,512]{2,1,0:T(8,128)}), f32[2,128,512]{2,1,0:T(8,128)}) %reduce-scatter.2.cloned.1.call-update) | async-done | bytes 524304 | tf_op jit(solution)/shard_map/reduce_scatter | solution.py:41
  52.2 1.1 pad_maximum_fusion.3
  53.3 8.1 %collective-permute-start = (f32[130,512]{1,0:T(8,128)S(1)}, f32[130,512]{1,0:T(8,128)S(1)}, u32[]{:S(2)}, u32[]{:S(2)}) collective-permute-start(f32[130,512]{1,0:T(8,128)S(1)} %slice_bitcast_fusion.3), channel_id=1, source_target_pairs={{4,0},{8,4},{12,8},{16,12},{20,16},{24,20},{28,24},{32,28},{36,32}... | collective-permute-start | bytes 798728 | tf_op jit(solution)/shard_map/ppermute | solution.py:16
  61.4 5.6 %collective-permute-done = f32[130,512]{1,0:T(8,128)S(1)} collective-permute-done((f32[130,512]{1,0:T(8,128)S(1)}, f32[130,512]{1,0:T(8,128)S(1)}, u32[]{:S(2)}, u32[]{:S(2)}) %collective-permute-start) | collective-permute-done | bytes 266272 | tf_op jit(solution)/shard_map/ppermute | solution.py:16
  68.1 1.4 fusion.17
  69.5 29.0 %all-gather.2.cloned.1.call-done = f32[512,512]{1,0:T(8,128)} async-done(((f32[128,512]{1,0:T(8,128)}), f32[512,512]{1,0:T(8,128)}) %all-gather.2.cloned.1.call-update) | async-done | bytes 1048592 | tf_op jit(solution)/shard_map/all_gather | solution.py:53
  98.5 8.8 %gather_fusion = f32[512]{0:T(512)S(1)} fusion(f32[512,512]{1,0:T(8,128)} %all-gather.2.cloned.1.call-done, s32[512]{0:T(512)S(1)} %bitcast.69), kind=kCustom, calls=%fused_computation | custom fusion | bytes 8192 | tf_op jit(solution)/shard_map/jit(diagonal)/cond/branch_0_fun/gather | solution.py:55
  110.3 1.2 select_subtract_fusion.3
  112.4 1.9 %fusion.18 = f32[512,512]{1,0:T(8,128)S(1)} fusion(f32[512,512]{1,0:T(8,128)S(1)} %select_subtract_fusion.3, f32[512,512]{1,0:T(8,128)S(1)} %copy-done, f32[]{:T(128)S(6)} %sqrt.6, f32[]{:T(128)S(6)} %add.37), kind=kOutput, calls=%fused_computation.41 | convolution fusion | flops 1611923456 | bytes 3145736 | tf_op jit(solution)/shard_map/dot_general | solution.py:20
  114.3 1.8 %select_subtract_fusion.2 = f32[512,512]{1,0:T(8,128)S(1)} fusion(f32[512,512]{1,0:T(8,128)S(1)} %fusion.13, f32[512,512]{1,0:T(8,128)S(1)} %fusion.18), kind=kOutput, calls=%fused_computation.14 | convolution fusion | flops 1611661312 | bytes 3145728 | tf_op jit(solution)/shard_map/dot_general | solution.py:20
  116.2 1.8 %fusion.33 = f32[512,512]{1,0:T(8,128)S(1)} fusion(f32[512,512]{1,0:T(8,128)S(1)} %select_subtract_fusion.2, f32[512,512]{1,0:T(8,128)S(1)} %fusion.18), kind=kOutput, calls=%fused_computation.64 | convolution fusion | flops 1610612736 | bytes 3145728 | tf_op jit(solution)/shard_map/dot_general | solution.py:20
  118.1 1.8 %fusion.32 = f32[512,512]{1,0:T(8,128)S(1)} fusion(f32[512,512]{1,0:T(8,128)S(1)} %select_subtract_fusion.2, f32[512,512]{1,0:T(8,128)S(1)} %fusion.13), kind=kOutput, calls=%fused_computation.63 | convolution fusion | flops 1610612736 | bytes 3145728 | tf_op jit(solution)/shard_map/dot_general | solution.py:20
  119.9 1.9 %select_subtract_fusion.1 = f32[512,512]{1,0:T(8,128)S(1)} fusion(f32[512,512]{1,0:T(8,128)S(1)} %fusion.32, f32[512,512]{1,0:T(8,128)S(1)} %fusion.33), kind=kOutput, calls=%fused_computation.13 | convolution fusion | flops 1611661312 | bytes 3145728 | tf_op jit(solution)/shard_map/dot_general | solution.py:20
  121.8 2.1 %fusion.34 = f32[512,512]{1,0:T(8,128)S(1)} fusion(f32[512,512]{1,0:T(8,128)S(1)} %select_subtract_fusion.1, f32[512,512]{1,0:T(8,128)S(1)} %fusion.32), kind=kOutput, calls=%fused_computation.65 | convolution fusion | flops 1610612736 | bytes 3145728 | tf_op jit(solution)/shard_map/dot_general | solution.py:20
  123.9 1.8 %fusion.35 = f32[512,512]{1,0:T(8,128)S(1)} fusion(f32[512,512]{1,0:T(8,128)S(1)} %select_subtract_fusion.1, f32[512,512]{1,0:T(8,128)S(1)} %fusion.33), kind=kOutput, calls=%fused_computation.66 | convolution fusion | flops 1610612736 | bytes 3145728 | tf_op jit(solution)/shard_map/dot_general | solution.py:20
  125.7 1.8 %select_subtract_fusion = f32[512,512]{1,0:T(8,128)S(1)} fusion(f32[512,512]{1,0:T(8,128)S(1)} %fusion.34, f32[512,512]{1,0:T(8,128)S(1)} %fusion.35), kind=kOutput, calls=%fused_computation.12 | convolution fusion | flops 1611661312 | bytes 3145728 | tf_op jit(solution)/shard_map/dot_general | solution.py:20
  127.6 1.9 %fusion.8 = bf16[512,512]{1,0:T(8,128)(2,1)S(1)} fusion(f32[512,512]{1,0:T(8,128)S(1)} %select_subtract_fusion, f32[512,512]{1,0:T(8,128)S(1)} %fusion.34, f32[]{:T(128)S(6)} %sqrt.7), kind=kOutput, calls=%fused_computation.21 | convolution fusion | flops 1611137024 | bytes 2621444 | tf_op jit(solution)/shard_map/dot_general | solution.py:20
  129.5 4.3 %collective-permute-start.1 = (bf16[513,512]{1,0:T(8,128)(2,1)S(1)}, bf16[513,512]{1,0:T(8,128)(2,1)S(1)}, u32[]{:S(2)}, u32[]{:S(2)}) collective-permute-start(bf16[513,512]{1,0:T(8,128)(2,1)S(1)} %pad_maximum_fusion.4), channel_id=1, source_target_pairs={{0,4},{4,8},{8,12},{12,16},{16,20},{20,24},{24,28},{28,32},{32,36}... | collective-permute-start | bytes 1575944 | tf_op jit(solution)/shard_map/ppermute | solution.py:16
  133.8 15.9 %collective-permute-done.1 = bf16[513,512]{1,0:T(8,128)(2,1)S(1)} collective-permute-done((bf16[513,512]{1,0:T(8,128)(2,1)S(1)}, bf16[513,512]{1,0:T(8,128)(2,1)S(1)}, u32[]{:S(2)}, u32[]{:S(2)}) %collective-permute-start.1) | collective-permute-done | bytes 525344 | tf_op jit(solution)/shard_map/ppermute | solution.py:16
  149.8 1.3 convolution_bitcast_fusion
  151.7 1.3 copy.9
  (34 shorter events, 5.7 us)
Async XLA Ops:
  6.5 2.5 %copy-start.1 = (bf16[1024,512]{1,0:T(8,128)(2,1)S(1)}, bf16[1024,512]{1,0:T(8,128)(2,1)}, u32[]{:S(2)}) copy-start(bf16[1024,512]{1,0:T(8,128)(2,1)} %param.3) | copy-start | bytes 3145732
  6.5 2.3 %copy-start.2 = (s32[1024]{0:T(1024)S(1)}, s32[1024]{0:T(1024)}, u32[]{:S(2)}) copy-start(s32[1024]{0:T(1024)} %param.4) | copy-start | bytes 12292
  6.5 45.6 %reduce-scatter.2.cloned.1.call-start = ((), (), s32[]{:S(2)}) async-start(), calls=%async_computation.1 | async-start | bytes 2621440 | tf_op jit(solution)/shard_map/reduce_scatter | solution.py:41
  11.6 86.9 %all-gather.2.cloned.1.call-start = ((), (), s32[]{:S(2)}) async-start(), calls=%async_computation.2 | async-start | bytes 1310720 | tf_op jit(solution)/shard_map/all_gather | solution.py:53
  53.3 13.6 %collective-permute-start = (f32[130,512]{1,0:T(8,128)S(1)}, f32[130,512]{1,0:T(8,128)S(1)}, u32[]{:S(2)}, u32[]{:S(2)}) collective-permute-start(f32[130,512]{1,0:T(8,128)S(1)} %slice_bitcast_fusion.3), channel_id=1, source_target_pairs={{4,0},{8,4},{12,8},{16,12},{20,16},{24,20},{28,24},{32,28},{36,32}... | collective-permute-start | bytes 798728 | tf_op jit(solution)/shard_map/ppermute | solution.py:16
  98.5 10.1 %copy-start = (f32[512,512]{1,0:T(8,128)S(1)}, f32[512,512]{1,0:T(8,128)}, u32[]{:S(2)}) copy-start(f32[512,512]{1,0:T(8,128)} %all-gather.2.cloned.1.call-done) | copy-start | bytes 3145732
  129.5 20.3 %collective-permute-start.1 = (bf16[513,512]{1,0:T(8,128)(2,1)S(1)}, bf16[513,512]{1,0:T(8,128)(2,1)S(1)}, u32[]{:S(2)}, u32[]{:S(2)}) collective-permute-start(bf16[513,512]{1,0:T(8,128)(2,1)S(1)} %pad_maximum_fusion.4), channel_id=1, source_target_pairs={{0,4},{4,8},{8,12},{12,16},{16,20},{20,24},{24,28},{28,32},{32,36}... | collective-permute-start | bytes 1575944 | tf_op jit(solution)/shard_map/ppermute | solution.py:16
Sparse Core Ops, SparseCore 0:
  11.8 40.3 reduce-scatter.1
  69.6 28.8 all-gather.1
where the time goes:
time: 161 us; the launch traced here: 160 us
  waiting for transfers between devices  85 us (53%)
  matrix products  23.5 us (15%)
  between operations  15 us (9%)
  starting transfers between devices  12.4 us (8%)
  local copies, waits for them, and re-layouts  12.3 us (8%)
  other arithmetic  5.89 us (4%)
  blocking collectives  5.77 us (4%)
    reduce_scatter x1, waiting for transfers between devices, shards(): lax.psum_scatter(gram_blocks, 'narrow', scatter_dimension=1, tiled=True)  34.4 us
    all_gather x1, waiting for transfers between devices, shards(): covariance = lax.all_gather(covariance_rows, 'narrow', axis=0, tiled=True)  29 us
    ppermute x2, waiting for transfers between devices, from_behind(): lax.ppermute(value, axis, [(source, source + steps) for source in range(f...  21.5 us
    dot_general x11, matrix products, highest_dot(): return jnp.dot(left, right, precision=lax.Precision.HIGHEST)  19.1 us
    ppermute x2, starting transfers between devices, from_behind(): lax.ppermute(value, axis, [(source, source + steps) for source in range(f...  12.4 us
    gather x1, local copies, waits for them, and re-layouts, shards(): trace_sum = jnp.sum(jnp.diagonal(covariance))  8.85 us
    psum x1, blocking collectives, shards(): sums_total, counts_total = lax.psum((column_sums, counts), 'narrow')  5.77 us
  transfers between devices with their start and end apart: 4, of which 4 were waited for; matrix products, arithmetic and copies ran while one was open for 0% of the time, Pallas kernels for 0%

commit v1 on v0

v1 whole, which is shorter than its diff:
```python
import jax
import jax.numpy as jnp
from jax import lax
from jax.experimental import pallas as pl
from jax.experimental.pallas import tpu as pltpu
from jax.sharding import Mesh
from jax.sharding import PartitionSpec as P

ROWS = 1024
F = 512
CONTROLS = 93
BLOCK = 96
LANES = 128
SUBROWS = ROWS // LANES
MEMBERS = 4
GROUPS = 128
PACK = F + 16

shrink = 0.1
epsilon = 1e-05
f32 = jnp.float32
bf16 = jnp.bfloat16
VMEM_LIMIT = 48 * 1024 * 1024


def matmul(left, right):
    return jnp.dot(left, right, preferred_element_type=f32)


def matmul_tn(left, right):
    return lax.dot_general(left, right, (((0,), (0,)), ((), ())), preferred_element_type=f32)


def pick_kernel(cells_hbm, plate_ref, control_ref, out_ref, cells, sems):
    chunk = ROWS // 4
    copies = [
        pltpu.make_async_copy(
            cells_hbm.at[pl.ds(part * chunk, chunk)], cells.at[pl.ds(part * chunk, chunk)], sems.at[part]
        )
        for part in range(4)
    ]
    for copy in copies:
        copy.start()
    group = lax.axis_index("d") // MEMBERS
    is_control = control_ref[...] == 1
    flags = is_control.astype(f32)
    upper = lax.broadcasted_iota(jnp.int32, (LANES, LANES), 0) <= lax.broadcasted_iota(
        jnp.int32, (LANES, LANES), 1
    )
    inclusive = matmul(flags.astype(bf16), upper.astype(f32).astype(bf16))
    total = jnp.broadcast_to(jnp.sum(flags, axis=1, keepdims=True), (SUBROWS, LANES))
    sub = lax.broadcasted_iota(jnp.int32, (SUBROWS, LANES), 0)
    running = total
    for step in (1, 2, 4):
        running = running + jnp.where(sub >= step, pltpu.roll(running, step, 0), 0.0)
    rank = jnp.where(is_control, inclusive + (running - total) - 1.0, -1.0).astype(jnp.int32)
    slots = lax.broadcasted_iota(jnp.int32, (BLOCK, LANES), 0)
    chosen = jnp.concatenate(
        [
            jnp.where(slots == jnp.broadcast_to(rank[k : k + 1, :], (BLOCK, LANES)), 1.0, 0.0).astype(bf16)
            for k in range(SUBROWS)
        ],
        axis=1,
    )
    earlier = jnp.sum(jnp.where(is_control & (plate_ref[...] < group), 1.0, 0.0), keepdims=True)
    picked = None
    for part, copy in enumerate(copies):
        copy.wait()
        span = slice(part * chunk, (part + 1) * chunk)
        term = matmul(chosen[:, span], cells[span, :])
        picked = term if picked is None else picked + term
    last = lax.broadcasted_iota(jnp.int32, (BLOCK, F), 0) == BLOCK - 1
    out_ref[...] = jnp.where(last, jnp.broadcast_to(earlier, (BLOCK, F)), picked).astype(bf16)


def sphere_kernel(rows_ref, out_ref):
    index = lax.axis_index("d")
    last_home = (index // MEMBERS == GROUPS - 1) & (index % 2 == 1)
    slot = lax.broadcasted_iota(jnp.int32, (BLOCK, F), 0).astype(f32)
    blocks = []
    count = jnp.zeros((1, 1), f32)
    for block in range(2 * MEMBERS):
        values = rows_ref[block * BLOCK : (block + 1) * BLOCK, :].astype(f32)
        earlier = values[BLOCK - 1 : BLOCK, 0:1]
        if block < MEMBERS:
            keep = (slot >= earlier) & (slot < float(CONTROLS))
            count = count + (float(CONTROLS) - earlier)
        else:
            earlier = jnp.where(last_home, 0.0, earlier)
            keep = slot < earlier
            count = count + earlier
        blocks.append(jnp.where(keep, values, 0.0).astype(bf16))
    picked = jnp.concatenate(blocks, axis=0)
    scale = 1.0 / jnp.maximum(count, 1.0)
    centre_row = matmul(jnp.ones((16, 2 * MEMBERS * BLOCK), bf16), picked)[0:1, :] * scale
    centre_column = matmul_tn(picked, jnp.ones((2 * MEMBERS * BLOCK, LANES), bf16))[:, 0:1] * scale
    gram = matmul_tn(picked, picked)
    covariance = gram * scale - centre_column * centre_row
    diagonal = lax.broadcasted_iota(jnp.int32, (F, F), 0) == lax.broadcasted_iota(jnp.int32, (F, F), 1)
    trace = jnp.sum(jnp.where(diagonal, covariance, 0.0), keepdims=True)
    ridge = shrink * trace / F + epsilon
    shrunk = (1.0 - shrink) * covariance + jnp.where(diagonal, ridge, 0.0)
    norm_scale = jnp.sqrt(jnp.sum(shrunk * shrunk, keepdims=True))
    start = shrunk * (1.0 / norm_scale)
    start_b = start.astype(bf16)
    square = matmul(start_b, start_b)
    iterate = 1.5 * start - 0.5 * square
    product = matmul((0.25 * square - 1.5 * start).astype(bf16), iterate.astype(bf16))
    rest = -0.75 * start - 0.5 * (2.25 * iterate + product)
    z = 2.25
    for step in range(2):
        rest_b = rest.astype(bf16)
        square = matmul(rest_b, rest_b)
        iterate = z * start + matmul(start_b, rest_b)
        product = z * z * iterate + matmul((2.0 * z * rest + square).astype(bf16), iterate.astype(bf16))
        rest = 1.5 * rest - 0.5 * product
        z = 1.5 * z
    inverse = rest + jnp.where(diagonal, z, 0.0)
    out_ref[0:F, :] = (inverse * (1.0 / jnp.sqrt(norm_scale))).astype(bf16)
    out_ref[F:PACK, :] = jnp.broadcast_to(centre_row, (PACK - F, F)).astype(bf16)


def apply_kernel(cells_ref, plate_ref, spheres_ref, out_hbm, out, sems):
    group = lax.axis_index("d") // MEMBERS
    earlier = jnp.sum(jnp.where(plate_ref[...] < group, 1.0, 0.0), keepdims=True)
    offsets = [
        matmul(spheres_ref[s * PACK + F : (s + 1) * PACK, :], spheres_ref[s * PACK : s * PACK + F, :])[0:1, :]
        for s in range(2)
    ]
    chunk = ROWS // 4
    copies = []
    for part in range(4):
        rows = cells_ref[part * chunk : (part + 1) * chunk, :]
        index = lax.broadcasted_iota(jnp.int32, (chunk, F), 0).astype(f32) + float(part * chunk)
        before = matmul(rows, spheres_ref[0:F, :]) - offsets[0]
        own = matmul(rows, spheres_ref[PACK : PACK + F, :]) - offsets[1]
        out[part * chunk : (part + 1) * chunk, :] = jnp.where(index < earlier, before, own).astype(bf16)
        copy = pltpu.make_async_copy(
            out.at[pl.ds(part * chunk, chunk)], out_hbm.at[pl.ds(part * chunk, chunk)], sems.at[part]
        )
        copy.start()
        copies.append(copy)
    for copy in copies:
        copy.wait()


def pairs(kind):
    if kind == "chip":
        return [[2 * i, 2 * i + 1] for i in range(GROUPS * MEMBERS // 2)]
    near = [[4 * p + 3, 4 * p + 4] for p in range(GROUPS - 1)]
    far = [[4 * p + 1, 4 * p + 6] for p in range(GROUPS - 1)]
    return near + far + [[0, 2], [4 * GROUPS - 3, 4 * GROUPS - 1]]


def shards(cells, plate_id, control):
    vmem = pl.BlockSpec(memory_space=pltpu.VMEM)
    hbm = pl.BlockSpec(memory_space=pl.ANY)
    params = pltpu.CompilerParams(vmem_limit_bytes=VMEM_LIMIT)
    plates = plate_id.reshape(SUBROWS, LANES)
    block = pl.pallas_call(
        pick_kernel,
        out_shape=jax.ShapeDtypeStruct((BLOCK, F), bf16),
        in_specs=[hbm, vmem, vmem],
        out_specs=vmem,
        scratch_shapes=[pltpu.VMEM((ROWS, F), bf16), pltpu.SemaphoreType.DMA((4,))],
        compiler_params=params,
        name="pick_controls",
    )(cells, plates, control.reshape(SUBROWS, LANES))
    members = [[MEMBERS * g + m for m in range(MEMBERS)] for g in range(GROUPS)]
    group_rows = lax.all_gather(block, "d", axis_index_groups=members, tiled=True)
    plate_rows = lax.all_gather(group_rows, "d", axis_index_groups=pairs("plate"), tiled=True)
    sphere = pl.pallas_call(
        sphere_kernel,
        out_shape=jax.ShapeDtypeStruct((PACK, F), bf16),
        in_specs=[vmem],
        out_specs=vmem,
        scratch_shapes=[],
        compiler_params=params,
        name="sphere",
    )(plate_rows)
    spheres = lax.all_gather(sphere, "d", axis_index_groups=pairs("chip"), tiled=True)
    return pl.pallas_call(
        apply_kernel,
        out_shape=jax.ShapeDtypeStruct((ROWS, F), bf16),
        in_specs=[vmem, vmem, vmem],
        out_specs=hbm,
        scratch_shapes=[pltpu.VMEM((ROWS, F), bf16), pltpu.SemaphoreType.DMA((4,))],
        compiler_params=params,
        name="apply_spheres",
    )(cells, plates, spheres)


def solution(mesh):
    line = Mesh(mesh.devices.reshape(-1), ("d",))
    return jax.shard_map(
        shards,
        mesh=line,
        in_specs=(P("d", None), P("d"), P("d")),
        out_specs=P("d", None),
        check_vma=False,
    )
```

time: 161 us -> 71.7 us (0.45)
  the two profiles are of different devices: /device:TPU:25 before, /device:TPU:1 now
where the time goes in v1:
time: 71.7 us; the launch traced here: 71.4 us
  blocking collectives  26.2 us (37%)
  waiting for transfers between devices  19.5 us (27%)
  between operations  13.4 us (19%)
  Pallas kernels  8.54 us (12%)
  local copies, waits for them, and re-layouts  3.84 us (5%)
    all_gather x1, waiting for transfers between devices, shards(): lax.all_gather(sphere, 'd', axis_index_groups=pairs('chip'), tiled=True)  19.5 us
    all_gather x1, blocking collectives, shards(): lax.all_gather(group_rows, 'd', axis_index_groups=pairs('plate'), tiled=T...  13.3 us
    all_gather x1, blocking collectives, shards(): lax.all_gather(block, 'd', axis_index_groups=members, tiled=True)  12.9 us
    pallas_call x1, Pallas kernels, shards(): pl.pallas_call(sphere_kernel, out_shape=jax.ShapeDtypeStruct((PACK, F), b...  5.55 us
    unnamed x12, local copies, waits for them, and re-layouts  3.84 us
    pallas_call x1, Pallas kernels, shards(): pl.pallas_call(apply_kernel, out_shape=jax.ShapeDtypeStruct((ROWS, F), bf...  2.21 us
  transfers between devices with their start and end apart: 1, of which 1 were waited for; matrix products, arithmetic and copies ran while one was open for 0% of the time, Pallas kernels for 0%

profile of v1, /device:TPU:1, one launch (start us, length us, event | category | flops | bytes accessed | tf_op | source)
XLA Modules:
  0.0 71.4 jit_solution(8719564145439596862)
XLA Ops:
  6.5 0.0 all-gather.2.cloned.1.call-start
  6.5 0.0 copy-start
  6.5 1.2 %copy-done = bf16[1024,512]{1,0:T(8,128)(2,1)S(1)} copy-done((bf16[1024,512]{1,0:T(8,128)(2,1)S(1)}, bf16[1024,512]{1,0:T(8,128)(2,1)}, u32[]{:S(2)}) %copy-start) | copy-done | bytes 1048600
  7.8 0.0 copy-start.3
  7.8 0.7 copy-done.3
  8.4 0.0 copy-start.5
  8.5 0.7 copy-done.5
  9.1 0.8 %pick_controls.1 = bf16[96,512]{1,0:T(8,128)(2,1)S(1)} custom-call(bf16[1024,512]{1,0:T(8,128)(2,1)S(1)} %copy-done, s32[8,128]{1,0:T(8,128)S(1)} %bitcast.2, s32[8,128]{1,0:T(8,128)S(1)} %bitcast.4), custom_call_target="tpu_custom_call" | custom-call | tf_op jit(solution)/shard_map/pick_controls/pallas_call | solution.py:160
  9.9 12.9 %all_gather.9 = bf16[384,512]{1,0:T(8,128)(2,1)S(1)} all-gather(bf16[96,512]{1,0:T(8,128)(2,1)S(1)} %pick_controls.1), channel_id=1, replica_groups={{0,1,2,3},{4,5,6,7},{8,9,10,11},{12,13,14,15},{16,17,18,19},{20,21,22,2..., dimensions={0}, use_global_device_ids=true | all-gather | bytes 491520 | tf_op jit(solution)/shard_map/all_gather | solution.py:170
  22.8 13.3 %all_gather.10.rows_ref = bf16[768,512]{1,0:T(8,128)(2,1)S(1)} all-gather(bf16[384,512]{1,0:T(8,128)(2,1)S(1)} %all_gather.9), channel_id=1, replica_groups={{3,4},{7,8},{11,12},{15,16},{19,20},{23,24},{27,28},{31,32},{35,36},{39..., dimensions={0}, use_global_device_ids=true | all-gather | bytes 1179648 | tf_op jit(solution)/shard_map/all_gather | solution.py:171
  36.1 0.0 copy-start.1
  36.1 0.0 copy-start.4
  36.1 5.5 %sphere.1 = bf16[528,512]{1,0:T(8,128)(2,1)} custom-call(bf16[768,512]{1,0:T(8,128)(2,1)S(1)} %all_gather.10.rows_ref), custom_call_target="tpu_custom_call" | custom-call | tf_op jit(solution)/shard_map/sphere/pallas_call | solution.py:172
  41.6 0.0 all-gather.2.cloned.1.call-update
  41.7 19.5 %all-gather.2.cloned.1.call-done.spheres_ref = bf16[1056,512]{1,0:T(8,128)(2,1)} async-done(((bf16[528,512]{1,0:T(8,128)(2,1)}), bf16[1056,512]{1,0:T(8,128)(2,1)}) %all-gather.2.cloned.1.call-update) | async-done | bytes 1081360 | tf_op jit(solution)/shard_map/all_gather | solution.py:181
  61.1 0.0 copy-done.1
  61.1 0.0 copy-done.4
  61.1 0.0 copy-start.2
  61.1 1.2 %copy-done.2 = bf16[1056,512]{1,0:T(8,128)(2,1)S(1)} copy-done((bf16[1056,512]{1,0:T(8,128)(2,1)S(1)}, bf16[1056,512]{1,0:T(8,128)(2,1)}, u32[]{:S(2)}) %copy-start.2) | copy-done | bytes 1081368
  62.4 2.2 %apply_spheres.1 = bf16[1024,512]{1,0:T(8,128)(2,1)} custom-call(bf16[1024,512]{1,0:T(8,128)(2,1)S(1)} %copy-done.1, s32[8,128]{1,0:T(8,128)S(1)} %bitcast.3, bf16[1056,512]{1,0:T(8,128)(2,1)S(1)} %copy-done.2), custom_call_target="tpu_custom_call" | custom-call | tf_op jit(solution)/shard_map/apply_spheres/pallas_call | solution.py:182
Async XLA Ops:
  6.5 54.6 %all-gather.2.cloned.1.call-start = ((), (), s32[]{:S(2)}) async-start(), calls=%async_computation | async-start | bytes 1622016 | tf_op jit(solution)/shard_map/all_gather | solution.py:181
  6.5 1.2 %copy-start = (bf16[1024,512]{1,0:T(8,128)(2,1)S(1)}, bf16[1024,512]{1,0:T(8,128)(2,1)}, u32[]{:S(2)}) copy-start(bf16[1024,512]{1,0:T(8,128)(2,1)} %cells_ref.1) | copy-start | bytes 3145732
  7.8 0.7 copy-start.3
  8.4 0.7 copy-start.5
  36.1 25.0 %copy-start.1 = (bf16[1024,512]{1,0:T(8,128)(2,1)S(1)}, bf16[1024,512]{1,0:T(8,128)(2,1)}, u32[]{:S(2)}) copy-start(bf16[1024,512]{1,0:T(8,128)(2,1)} %cells_ref.1) | copy-start | bytes 3145732
  36.1 25.1 %copy-start.4 = (s32[1024]{0:T(1024)S(1)}, s32[1024]{0:T(1024)}, u32[]{:S(2)}) copy-start(s32[1024]{0:T(1024)} %param.4) | copy-start | bytes 12292
  61.1 1.2 %copy-start.2 = (bf16[1056,512]{1,0:T(8,128)(2,1)S(1)}, bf16[1056,512]{1,0:T(8,128)(2,1)}, u32[]{:S(2)}) copy-start(bf16[1056,512]{1,0:T(8,128)(2,1)} %all-gather.2.cloned.1.call-done.spheres_ref) | copy-start | bytes 3244036
Sparse Core Ops, SparseCore 0:
  41.8 19.3 all-gather.1

commit v2 on v1

v2 whole, which is shorter than its diff:
```python
import jax
import jax.numpy as jnp
from jax import lax
from jax.experimental import pallas as pl
from jax.experimental.pallas import tpu as pltpu
from jax.sharding import Mesh
from jax.sharding import PartitionSpec as P

ROWS = 1024
F = 512
CONTROLS = 93
BLOCK = 96
LANES = 128
SUBROWS = ROWS // LANES
MEMBERS = 4
CHUNKS = 4
HOME = 3 * BLOCK
GROUPS = 128
HALF = F // 2
CENTRE = HALF + HALF // 2
PACK = CENTRE + 16

shrink = 0.1
epsilon = 1e-05
f32 = jnp.float32
bf16 = jnp.bfloat16
VMEM_LIMIT = 48 * 1024 * 1024


def matmul(left, right):
    return jnp.dot(left, right, preferred_element_type=f32)


def matmul_tn(left, right):
    return lax.dot_general(left, right, (((0,), (0,)), ((), ())), preferred_element_type=f32)


def pick_kernel(cells_hbm, plate_hbm, control_hbm, out_ref, cells, plate_ref, control_ref, sems, flag_sems):
    chunk = ROWS // 4
    flag_copies = [
        pltpu.make_async_copy(control_hbm, control_ref, flag_sems.at[0]),
        pltpu.make_async_copy(plate_hbm, plate_ref, flag_sems.at[1]),
    ]
    copies = [
        pltpu.make_async_copy(
            cells_hbm.at[pl.ds(part * chunk, chunk)], cells.at[pl.ds(part * chunk, chunk)], sems.at[part]
        )
        for part in range(4)
    ]
    for copy in flag_copies + copies:
        copy.start()
    group = lax.axis_index("d") // MEMBERS
    for copy in flag_copies:
        copy.wait()
    is_control = control_ref[...] == 1
    flags = is_control.astype(f32)
    upper = lax.broadcasted_iota(jnp.int32, (LANES, LANES), 0) <= lax.broadcasted_iota(
        jnp.int32, (LANES, LANES), 1
    )
    inclusive = matmul(flags.astype(bf16), upper.astype(f32).astype(bf16))
    total = jnp.broadcast_to(jnp.sum(flags, axis=1, keepdims=True), (SUBROWS, LANES))
    sub = lax.broadcasted_iota(jnp.int32, (SUBROWS, LANES), 0)
    running = total
    for step in (1, 2, 4):
        running = running + jnp.where(sub >= step, pltpu.roll(running, step, 0), 0.0)
    rank = jnp.where(is_control, inclusive + (running - total) - 1.0, -1.0).astype(jnp.int32)
    slots = lax.broadcasted_iota(jnp.int32, (BLOCK, LANES), 0)
    chosen = jnp.concatenate(
        [
            jnp.where(slots == jnp.broadcast_to(rank[k : k + 1, :], (BLOCK, LANES)), 1.0, 0.0).astype(bf16)
            for k in range(SUBROWS)
        ],
        axis=1,
    )
    earlier = jnp.sum(jnp.where(is_control & (plate_ref[...] < group), 1.0, 0.0), keepdims=True)
    picked = None
    for part, copy in enumerate(copies):
        copy.wait()
        span = slice(part * chunk, (part + 1) * chunk)
        term = matmul(chosen[:, span], cells[span, :])
        picked = term if picked is None else picked + term
    last = lax.broadcasted_iota(jnp.int32, (BLOCK, F), 0) == BLOCK - 1
    out_ref[...] = jnp.where(last, jnp.broadcast_to(earlier, (BLOCK, F)), picked).astype(bf16)


def sphere_kernel(rows_ref, group_ref, first_ref, out_ref, start_ref, rest_ref, start_b, rest_b, left_b, iterate_b):
    index = lax.axis_index("d")
    group = index // MEMBERS
    home = (group + index) % 2
    last_home = (group == GROUPS - 1) & (home == 1)
    first_plate = group + home == 1
    slot = lax.broadcasted_iota(jnp.int32, (BLOCK, F), 0).astype(f32)
    blocks = []
    count = jnp.zeros((1, 1), f32)
    for block in range(6):
        values = rows_ref[block * BLOCK : (block + 1) * BLOCK, :].astype(f32)
        earlier = values[BLOCK - 1 : BLOCK, 0:1]
        if block < 3:
            keep = (slot >= earlier) & (slot < float(CONTROLS))
            count = count + (float(CONTROLS) - earlier)
        else:
            earlier = jnp.where(last_home, 0.0, earlier)
            keep = slot < earlier
            count = count + earlier
        blocks.append(jnp.where(keep, values, 0.0).astype(bf16))
    opening = jnp.where(group == 0, group_ref[...].astype(f32), first_ref[...].astype(f32))
    blocks.append(jnp.where(first_plate & (slot < float(CONTROLS)), opening, 0.0).astype(bf16))
    count = count + jnp.where(first_plate, float(CONTROLS), 0.0)
    picked = jnp.concatenate(blocks, axis=0)
    scale = 1.0 / jnp.maximum(count, 1.0)
    centre_row = matmul(jnp.ones((16, 7 * BLOCK), bf16), picked)[0:1, :] * scale
    centre_column = matmul_tn(picked, jnp.ones((7 * BLOCK, LANES), bf16))[:, 0:1] * scale
    gram = matmul_tn(picked, picked)
    covariance = gram * scale - centre_column * centre_row
    diagonal = lax.broadcasted_iota(jnp.int32, (F, F), 0) == lax.broadcasted_iota(jnp.int32, (F, F), 1)
    trace = jnp.sum(jnp.where(diagonal, covariance, 0.0), keepdims=True)
    ridge = shrink * trace / F + epsilon
    shrunk = (1.0 - shrink) * covariance + jnp.where(diagonal, ridge, 0.0)
    norm_scale = jnp.sqrt(jnp.sum(shrunk * shrunk, keepdims=True))
    start = shrunk * (1.0 / norm_scale)
    start_ref[...] = start
    start_b[...] = start.astype(bf16)
    parts = [slice(k * HALF, (k + 1) * HALF) for k in range(2)]
    for part in parts:
        a = start_ref[part, :]
        square = matmul(start_b[part, :], start_b[...])
        iterate = 1.5 * a - 0.5 * square
        left_b[part, :] = (0.25 * square - 1.5 * a).astype(bf16)
        iterate_b[part, :] = iterate.astype(bf16)
        rest_ref[part, :] = -0.75 * a - 1.125 * iterate
    z = 2.25
    for step in range(2):
        for part in parts:
            rest = rest_ref[part, :] - 0.5 * matmul(left_b[part, :], iterate_b[...])
            rest_ref[part, :] = rest
            rest_b[part, :] = rest.astype(bf16)
        for part in parts:
            rest = rest_ref[part, :]
            square = matmul(rest_b[part, :], rest_b[...])
            iterate = z * start_ref[part, :] + matmul(start_b[part, :], rest_b[...])
            left_b[part, :] = (2.0 * z * rest + square).astype(bf16)
            iterate_b[part, :] = iterate.astype(bf16)
            rest_ref[part, :] = 1.5 * rest - (0.5 * z * z) * iterate
        z = 1.5 * z
    rest = jnp.concatenate([rest_ref[part, :] - 0.5 * matmul(left_b[part, :], iterate_b[...]) for part in parts], axis=0)
    inverse = rest + jnp.where(diagonal, z, 0.0)
    sphere = (inverse * (1.0 / jnp.sqrt(norm_scale))).astype(bf16)
    out_ref[0:HALF, :] = sphere[0:HALF, :]
    out_ref[HALF:CENTRE, 0:HALF] = sphere[HALF : HALF + HALF // 2, HALF:F]
    out_ref[HALF:CENTRE, HALF:F] = sphere[HALF + HALF // 2 : F, HALF:F]
    out_ref[CENTRE:PACK, :] = jnp.broadcast_to(centre_row, (PACK - CENTRE, F)).astype(bf16)


def apply_kernel(cells_ref, plate_ref, packed_ref, out_hbm, out, spheres, sems):
    group = lax.axis_index("d") // MEMBERS
    parity = group % 2
    earlier = jnp.sum(jnp.where(plate_ref[...] < group, 1, 0))
    offsets = []
    for side, core in enumerate((parity, 1 - parity)):
        upper = packed_ref[core, 0:HALF, :]
        spheres[side, 0:HALF, :] = upper
        spheres[side, HALF:F, 0:HALF] = upper[:, HALF:F].T
        spheres[side, HALF:CENTRE, HALF:F] = packed_ref[core, HALF:CENTRE, 0:HALF]
        spheres[side, CENTRE:F, HALF:F] = packed_ref[core, HALF:CENTRE, HALF:F]
        offsets.append(matmul(packed_ref[core, CENTRE:PACK, :], spheres[side])[0:1, :])
    chunk = ROWS // CHUNKS
    copies = []
    for part in range(CHUNKS):
        start = part * chunk
        span = slice(start, start + chunk)
        side = jnp.where(earlier > start, 0, 1)
        offset = jnp.where(earlier > start, offsets[0], offsets[1])
        out[span, :] = (matmul(cells_ref[span, :], spheres[side]) - offset).astype(bf16)

        @pl.when((earlier > start) & (earlier < start + chunk))
        def _(start=start, span=span):
            index = lax.broadcasted_iota(jnp.int32, (chunk, F), 0) + start
            own = matmul(cells_ref[span, :], spheres[1]) - offsets[1]
            out[span, :] = jnp.where(index < earlier, out[span, :].astype(f32), own).astype(bf16)

        copy = pltpu.make_async_copy(out.at[pl.ds(start, chunk)], out_hbm.at[pl.ds(start, chunk)], sems.at[part])
        copy.start()
        copies.append(copy)
    for copy in copies:
        copy.wait()


def pairs(kind):
    if kind == "chip":
        return [[2 * i, 2 * i + 1] for i in range(GROUPS * MEMBERS // 2)]
    first = [MEMBERS * p + 1 - p % 2 for p in range(GROUPS)]
    near = [[d + 2, d + 4] for d in first[:-1]]
    far = [[d, d + 6] for d in first[:-1]]
    return near + far + [[0, 2], [first[-1], first[-1] + 2]]


def shards(cells, plate_id, control):
    vmem = pl.BlockSpec(memory_space=pltpu.VMEM)
    hbm = pl.BlockSpec(memory_space=pltpu.HBM)
    params = pltpu.CompilerParams(vmem_limit_bytes=VMEM_LIMIT)
    plates = plate_id.reshape(SUBROWS, LANES)
    block = pl.pallas_call(
        pick_kernel,
        out_shape=jax.ShapeDtypeStruct((BLOCK, F), bf16),
        in_specs=[hbm, hbm, hbm],
        out_specs=vmem,
        scratch_shapes=[
            pltpu.VMEM((ROWS, F), bf16),
            pltpu.VMEM((SUBROWS, LANES), jnp.int32),
            pltpu.VMEM((SUBROWS, LANES), jnp.int32),
            pltpu.SemaphoreType.DMA((4,)),
            pltpu.SemaphoreType.DMA((2,)),
        ],
        name="pick_controls",
    )(cells, plates, control.reshape(SUBROWS, LANES))
    members = [[MEMBERS * g + m for m in range(MEMBERS)] for g in range(GROUPS)]
    group_rows = lax.all_gather(block, "d", axis_index_groups=members, tiled=True)
    index = lax.axis_index("d")
    home = lax.rem(index // MEMBERS + index, 2)
    side = lax.dynamic_slice_in_dim(group_rows, home * BLOCK, HOME, 0)
    opening = group_rows[0:BLOCK]
    first = lax.ppermute(opening, "d", [(0, 5), (2, 7)])
    plate_rows = lax.all_gather(side, "d", axis_index_groups=pairs("plate"), tiled=True)
    sphere = pl.pallas_call(
        sphere_kernel,
        out_shape=jax.ShapeDtypeStruct((PACK, F), bf16),
        in_specs=[vmem, vmem, vmem],
        out_specs=vmem,
        scratch_shapes=[pltpu.VMEM((F, F), f32)] * 2 + [pltpu.VMEM((F, F), bf16)] * 4,
        compiler_params=params,
        name="sphere",
    )(plate_rows, opening, first)
    spheres = lax.all_gather(sphere, "d", axis_index_groups=pairs("chip"), tiled=True)
    return pl.pallas_call(
        apply_kernel,
        out_shape=jax.ShapeDtypeStruct((ROWS, F), bf16),
        in_specs=[vmem, vmem, vmem],
        out_specs=hbm,
        scratch_shapes=[
            pltpu.VMEM((ROWS, F), bf16),
            pltpu.VMEM((2, F, F), bf16),
            pltpu.SemaphoreType.DMA((CHUNKS,)),
        ],
        compiler_params=params,
        name="apply_spheres",
    )(cells, plates, spheres.reshape(2, PACK, F))


def solution(mesh):
    line = Mesh(mesh.devices.reshape(-1), ("d",))
    return jax.shard_map(
        shards,
        mesh=line,
        in_specs=(P("d", None), P("d"), P("d")),
        out_specs=P("d", None),
        check_vma=False,
    )
```

time: 71.7 us -> 36.6 us (0.51)
  the two profiles are of different devices: /device:TPU:1 before, /device:TPU:25 now
where the time goes in v2:
time: 36.6 us; the launch traced here: 36.4 us
  blocking collectives  26.3 us (72%)
  Pallas kernels  9.33 us (25%)
  starting transfers between devices  0.67 us (2%)
    all_gather x1, blocking collectives, shards(): lax.all_gather(side, 'd', axis_index_groups=pairs('plate'), tiled=True)  9.68 us
    all_gather x1, blocking collectives, shards(): lax.all_gather(sphere, 'd', axis_index_groups=pairs('chip'), tiled=True)  9.44 us
    all_gather x1, blocking collectives, shards(): lax.all_gather(block, 'd', axis_index_groups=members, tiled=True)  7.18 us
    pallas_call x1, Pallas kernels, shards(): pl.pallas_call(sphere_kernel, out_shape=jax.ShapeDtypeStruct((PACK, F), b...  4.57 us
    pallas_call x1, Pallas kernels, shards(): pl.pallas_call(apply_kernel, out_shape=jax.ShapeDtypeStruct((ROWS, F), bf...  2.43 us
    pallas_call x1, Pallas kernels, shards(): pl.pallas_call(pick_kernel, out_shape=jax.ShapeDtypeStruct((BLOCK, F), bf...  2.32 us
  transfers between devices with their start and end apart: 1, of which 0 were waited for; matrix products, arithmetic and copies ran while one was open for 0% of the time, Pallas kernels for 0%

profile of v2, /device:TPU:25, one launch (start us, length us, event | category | flops | bytes accessed | tf_op | source)
XLA Modules:
  0.0 36.4 jit_solution(9865164990730629763)
XLA Ops:
  0.0 2.3 %pick_controls.1 = bf16[96,512]{1,0:T(8,128)(2,1)} custom-call(bf16[1024,512]{1,0:T(8,128)(2,1)} %cells_ref.1, s32[8,128]{1,0:T(8,128)} %bitcast.4, s32[8,128]{1,0:T(8,128)} %bitcast.6), custom_call_target="tpu_custom_call" | custom-call | tf_op jit(solution)/shard_map/pick_controls/pallas_call | solution.py:202
  2.3 7.2 %all_gather.9 = bf16[384,512]{1,0:T(8,128)(2,1)S(1)} all-gather(bf16[96,512]{1,0:T(8,128)(2,1)} %pick_controls.1), channel_id=1, replica_groups={{0,1,2,3},{4,5,6,7},{8,9,10,11},{12,13,14,15},{16,17,18,19},{20,21,22,2..., dimensions={0}, use_global_device_ids=true | all-gather | bytes 491520 | tf_op jit(solution)/shard_map/all_gather | solution.py:217
  9.5 0.7 %collective-permute-start = (bf16[96,512]{1,0:T(8,128)(2,1)S(1)}, bf16[96,512]{1,0:T(8,128)(2,1)S(1)}, u32[]{:S(2)}, u32[]{:S(2)}) collective-permute-start(bf16[96,512]{1,0:T(8,128)(2,1)S(1)} %slice.4.group_ref), channel_id=1, source_target_pairs={{0,5},{2,7}} | collective-permute-start | bytes 294920 | tf_op jit(solution)/shard_map/ppermute | solution.py:222
  10.3 9.7 %all_gather.10.rows_ref = bf16[576,512]{1,0:T(8,128)(2,1)S(1)} all-gather(bf16[288,512]{1,0:T(8,128)(2,1)S(1)} %constant_dynamic-slice_fusion), channel_id=1, replica_groups={{3,5},{6,8},{11,13},{14,16},{19,21},{22,24},{27,29},{30,32},{35,37},{38..., dimensions={0}, use_global_device_ids=true | all-gather | bytes 884736 | tf_op jit(solution)/shard_map/all_gather | solution.py:223
  19.9 0.0 copy-start
  19.9 0.0 collective-permute-done.first_ref
  19.9 4.6 %sphere.1 = bf16[400,512]{1,0:T(8,128)(2,1)S(1)} custom-call(bf16[576,512]{1,0:T(8,128)(2,1)S(1)} %all_gather.10.rows_ref, bf16[96,512]{1,0:T(8,128)(2,1)S(1)} %slice.4.group_ref, bf16[96,512]{1,0:T(8,128)(2,1)S(1)} %collective-permute-done.first_ref), custom_call_target="tpu_custom_call" | custom-call | tf_op jit(solution)/shard_map/sphere/pallas_call | solution.py:224
  24.5 0.0 copy-start.1
  24.5 9.4 %all_gather.11 = bf16[800,512]{1,0:T(8,128)(2,1)S(1)} all-gather(bf16[400,512]{1,0:T(8,128)(2,1)S(1)} %sphere.1), channel_id=1, replica_groups={{0,1},{2,3},{4,5},{6,7},{8,9},{10,11},{12,13},{14,15},{16,17},{18,19},{..., dimensions={0}, use_global_device_ids=true | all-gather | bytes 1228800 | tf_op jit(solution)/shard_map/all_gather | solution.py:233
  34.0 0.0 copy-done
  34.0 0.0 copy-done.1
  34.0 2.4 %apply_spheres.1 = bf16[1024,512]{1,0:T(8,128)(2,1)} custom-call(bf16[1024,512]{1,0:T(8,128)(2,1)S(1)} %copy-done, s32[8,128]{1,0:T(8,128)S(1)} %bitcast.5, bf16[2,400,512]{2,1,0:T(8,128)(2,1)S(1)} %bitcast.3), custom_call_target="tpu_custom_call" | custom-call | tf_op jit(solution)/shard_map/apply_spheres/pallas_call | solution.py:234
  (2 shorter events, 0.0 us)
Async XLA Ops:
  9.5 10.4 %collective-permute-start = (bf16[96,512]{1,0:T(8,128)(2,1)S(1)}, bf16[96,512]{1,0:T(8,128)(2,1)S(1)}, u32[]{:S(2)}, u32[]{:S(2)}) collective-permute-start(bf16[96,512]{1,0:T(8,128)(2,1)S(1)} %slice.4.group_ref), channel_id=1, source_target_pairs={{0,5},{2,7}} | collective-permute-start | bytes 294920 | tf_op jit(solution)/shard_map/ppermute | solution.py:222
  19.9 14.0 %copy-start = (bf16[1024,512]{1,0:T(8,128)(2,1)S(1)}, bf16[1024,512]{1,0:T(8,128)(2,1)}, u32[]{:S(2)}) copy-start(bf16[1024,512]{1,0:T(8,128)(2,1)} %cells_ref.1) | copy-start | bytes 3145732
  24.5 9.5 %copy-start.1 = (s32[1024]{0:T(1024)S(1)}, s32[1024]{0:T(1024)}, u32[]{:S(2)}) copy-start(s32[1024]{0:T(1024)} %param.4) | copy-start | bytes 12292

commit v3 on v2

--- a/solution.py
+++ b/solution.py
@@ -89,38 +89,54 @@
     home = (group + index) % 2
     last_home = (group == GROUPS - 1) & (home == 1)
     first_plate = group + home == 1
-    slot = lax.broadcasted_iota(jnp.int32, (BLOCK, F), 0).astype(f32)
+    slot = lax.broadcasted_iota(jnp.int32, (BLOCK, LANES), 0).astype(f32)
     blocks = []
     count = jnp.zeros((1, 1), f32)
+
+    def keep(rows, low, high):
+        flags = jnp.where((slot >= low) & (slot < high), 1.0, 0.0).astype(bf16)
+        blocks.append(rows * jnp.concatenate([flags] * (F // LANES), axis=1))
+
     for block in range(6):
-        values = rows_ref[block * BLOCK : (block + 1) * BLOCK, :].astype(f32)
-        earlier = values[BLOCK - 1 : BLOCK, 0:1]
+        earlier = rows_ref[(block + 1) * BLOCK - 16 : (block + 1) * BLOCK, 0:LANES].astype(f32)[15:16, 0:1]
         if block < 3:
-            keep = (slot >= earlier) & (slot < float(CONTROLS))
-            count = count + (float(CONTROLS) - earlier)
+            low, high = earlier, jnp.full((1, 1), float(CONTROLS), f32)
         else:
-            earlier = jnp.where(last_home, 0.0, earlier)
-            keep = slot < earlier
-            count = count + earlier
-        blocks.append(jnp.where(keep, values, 0.0).astype(bf16))
-    opening = jnp.where(group == 0, group_ref[...].astype(f32), first_ref[...].astype(f32))
-    blocks.append(jnp.where(first_plate & (slot < float(CONTROLS)), opening, 0.0).astype(bf16))
-    count = count + jnp.where(first_plate, float(CONTROLS), 0.0)
+            low, high = jnp.zeros((1, 1), f32), jnp.where(last_home, 0.0, earlier)
+        keep(rows_ref[block * BLOCK : (block + 1) * BLOCK, :], low, high)
+        count = count + (high - low)
+    opening = jnp.where(first_plate, float(CONTROLS), 0.0)
+    keep(jnp.where(group == 0, group_ref[...], first_ref[...]), 0.0, opening)
+    count = count + opening
     picked = jnp.concatenate(blocks, axis=0)
     scale = 1.0 / jnp.maximum(count, 1.0)
     centre_row = matmul(jnp.ones((16, 7 * BLOCK), bf16), picked)[0:1, :] * scale
-    centre_column = matmul_tn(picked, jnp.ones((7 * BLOCK, LANES), bf16))[:, 0:1] * scale
-    gram = matmul_tn(picked, picked)
-    covariance = gram * scale - centre_column * centre_row
-    diagonal = lax.broadcasted_iota(jnp.int32, (F, F), 0) == lax.broadcasted_iota(jnp.int32, (F, F), 1)
-    trace = jnp.sum(jnp.where(diagonal, covariance, 0.0), keepdims=True)
+    centre_column = jnp.broadcast_to(centre_row, (8, F)).T[:, 0:1]
+    parts = [slice(0, HALF), slice(HALF, F)]
+    quarters = [slice(k, k + LANES) for k in range(0, F, LANES)]
+    eye = lax.broadcasted_iota(jnp.int32, (LANES, LANES), 0) == lax.broadcasted_iota(jnp.int32, (LANES, LANES), 1)
+    squares = jnp.zeros((1, F), f32)
+    for part in parts:
+        covariance = matmul_tn(picked[:, part], picked) * scale - centre_column[part, :] * centre_row
+        start_ref[part, :] = covariance
+        squares = squares + jnp.sum(covariance * covariance, axis=0, keepdims=True)
+    traces = jnp.zeros((1, LANES), f32)
+    for span in quarters:
+        traces = traces + jnp.sum(jnp.where(eye, start_ref[span, span], 0.0), axis=0, keepdims=True)
+    trace = jnp.sum(traces, keepdims=True)
     ridge = shrink * trace / F + epsilon
-    shrunk = (1.0 - shrink) * covariance + jnp.where(diagonal, ridge, 0.0)
-    norm_scale = jnp.sqrt(jnp.sum(shrunk * shrunk, keepdims=True))
-    start = shrunk * (1.0 / norm_scale)
-    start_ref[...] = start
-    start_b[...] = start.astype(bf16)
-    parts = [slice(k * HALF, (k + 1) * HALF) for k in range(2)]
+    keep_part = 1.0 - shrink
+    norm_square = (
+        keep_part * keep_part * jnp.sum(squares, keepdims=True) + 2.0 * keep_part * ridge * trace + F * ridge * ridge
+    )
+    norm_scale = jnp.sqrt(norm_square)
+    inverse_norm = 1.0 / norm_scale
+    for part in parts:
+        start_ref[part, :] = start_ref[part, :] * (keep_part * inverse_norm)
+    for span in quarters:
+        start_ref[span, span] = start_ref[span, span] + jnp.where(eye, ridge * inverse_norm, 0.0)
+    for part in parts:
+        start_b[part, :] = start_ref[part, :].astype(bf16)
     for part in parts:
         a = start_ref[part, :]
         square = matmul(start_b[part, :], start_b[...])
@@ -136,18 +152,22 @@
             rest_b[part, :] = rest.astype(bf16)
         for part in parts:
             rest = rest_ref[part, :]
-            square = matmul(rest_b[part, :], rest_b[...])
-            iterate = z * start_ref[part, :] + matmul(start_b[part, :], rest_b[...])
+            both = matmul(jnp.concatenate([rest_b[part, :], start_b[part, :]], axis=0), rest_b[...])
+            square = both[0:HALF, :]
+            iterate = z * start_ref[part, :] + both[HALF:F, :]
             left_b[part, :] = (2.0 * z * rest + square).astype(bf16)
             iterate_b[part, :] = iterate.astype(bf16)
             rest_ref[part, :] = 1.5 * rest - (0.5 * z * z) * iterate
         z = 1.5 * z
-    rest = jnp.concatenate([rest_ref[part, :] - 0.5 * matmul(left_b[part, :], iterate_b[...]) for part in parts], axis=0)
-    inverse = rest + jnp.where(diagonal, z, 0.0)
-    sphere = (inverse * (1.0 / jnp.sqrt(norm_scale))).astype(bf16)
-    out_ref[0:HALF, :] = sphere[0:HALF, :]
-    out_ref[HALF:CENTRE, 0:HALF] = sphere[HALF : HALF + HALF // 2, HALF:F]
-    out_ref[HALF:CENTRE, HALF:F] = sphere[HALF + HALF // 2 : F, HALF:F]
+    gain = lax.rsqrt(norm_scale)
+    for span in quarters:
+        rest_ref[span, span] = rest_ref[span, span] + jnp.where(eye, z, 0.0)
+    upper, lower = parts
+    sphere = (rest_ref[upper, :] - 0.5 * matmul(left_b[upper, :], iterate_b[...])) * gain
+    out_ref[upper, :] = sphere.astype(bf16)
+    corner = (rest_ref[lower, lower] - 0.5 * matmul(left_b[lower, :], iterate_b[:, lower])) * gain
+    out_ref[HALF:CENTRE, 0:HALF] = corner[0 : HALF // 2, :].astype(bf16)
+    out_ref[HALF:CENTRE, HALF:F] = corner[HALF // 2 : HALF, :].astype(bf16)
     out_ref[CENTRE:PACK, :] = jnp.broadcast_to(centre_row, (PACK - CENTRE, F)).astype(bf16)
 
 
@@ -164,20 +184,19 @@
         spheres[side, CENTRE:F, HALF:F] = packed_ref[core, HALF:CENTRE, HALF:F]
         offsets.append(matmul(packed_ref[core, CENTRE:PACK, :], spheres[side])[0:1, :])
     chunk = ROWS // CHUNKS
+    mixed = jnp.minimum(earlier // chunk, CHUNKS - 1)
+    rows = cells_ref[pl.ds(pl.multiple_of(mixed * chunk, chunk), chunk), :]
+    own = matmul(rows, spheres[1]) - offsets[1]
+    slot = lax.broadcasted_iota(jnp.int32, (chunk, F), 0)
     copies = []
     for part in range(CHUNKS):
         start = part * chunk
         span = slice(start, start + chunk)
         side = jnp.where(earlier > start, 0, 1)
         offset = jnp.where(earlier > start, offsets[0], offsets[1])
-        out[span, :] = (matmul(cells_ref[span, :], spheres[side]) - offset).astype(bf16)
-
-        @pl.when((earlier > start) & (earlier < start + chunk))
-        def _(start=start, span=span):
-            index = lax.broadcasted_iota(jnp.int32, (chunk, F), 0) + start
-            own = matmul(cells_ref[span, :], spheres[1]) - offsets[1]
-            out[span, :] = jnp.where(index < earlier, out[span, :].astype(f32), own).astype(bf16)
-
+        values = matmul(cells_ref[span, :], spheres[side]) - offset
+        limit = jnp.where(mixed == part, earlier - start, chunk)
+        out[span, :] = jnp.where(slot < limit, values, own).astype(bf16)
         copy = pltpu.make_async_copy(out.at[pl.ds(start, chunk)], out_hbm.at[pl.ds(start, chunk)], sems.at[part])
         copy.start()
         copies.append(copy)
@@ -211,12 +230,13 @@
             pltpu.SemaphoreType.DMA((4,)),
             pltpu.SemaphoreType.DMA((2,)),
         ],
+        compiler_params=params,
         name="pick_controls",
-    )(cells, plates, control.reshape(SUBROWS, LANES))
+    )(*(pltpu.with_memory_space_constraint(x, pltpu.HBM) for x in (cells, plates, control.reshape(SUBROWS, LANES))))
     members = [[MEMBERS * g + m for m in range(MEMBERS)] for g in range(GROUPS)]
     group_rows = lax.all_gather(block, "d", axis_index_groups=members, tiled=True)
     index = lax.axis_index("d")
-    home = lax.rem(index // MEMBERS + index, 2)
+    home = (index ^ (index >> 2)) & 1
     side = lax.dynamic_slice_in_dim(group_rows, home * BLOCK, HOME, 0)
     opening = group_rows[0:BLOCK]
     first = lax.ppermute(opening, "d", [(0, 5), (2, 7)])

time: 36.6 us -> 34.3 us (0.937)
  Pallas kernels: 9.33 us -> 7.31 us
    pallas_call x1, Pallas kernels: 4.57 us -> 3.84 us  [shards(): pl.pallas_call(sphere_kernel, out_shape=jax.ShapeDtypeStruct((PACK, F), b...]
    pallas_call x1, Pallas kernels: 2.43 us -> 1.79 us  [shards(): pl.pallas_call(apply_kernel, out_shape=jax.ShapeDtypeStruct((ROWS, F), bf...]
    pallas_call x1, Pallas kernels: 2.32 us -> 1.69 us  [shards(): pl.pallas_call(pick_kernel, out_shape=jax.ShapeDtypeStruct((BLOCK, F), bf...]
where the time goes in v3:
time: 34.3 us; the launch traced here: 34.1 us
  blocking collectives  26.1 us (76%)
  Pallas kernels  7.31 us (21%)
  starting transfers between devices  0.67 us (2%)
    all_gather x1, blocking collectives, shards(): lax.all_gather(side, 'd', axis_index_groups=pairs('plate'), tiled=True)  9.67 us
    all_gather x1, blocking collectives, shards(): lax.all_gather(sphere, 'd', axis_index_groups=pairs('chip'), tiled=True)  9.41 us
    all_gather x1, blocking collectives, shards(): lax.all_gather(block, 'd', axis_index_groups=members, tiled=True)  6.97 us
    pallas_call x1, Pallas kernels, shards(): pl.pallas_call(sphere_kernel, out_shape=jax.ShapeDtypeStruct((PACK, F), b...  3.84 us
    pallas_call x1, Pallas kernels, shards(): pl.pallas_call(apply_kernel, out_shape=jax.ShapeDtypeStruct((ROWS, F), bf...  1.79 us
    pallas_call x1, Pallas kernels, shards(): pl.pallas_call(pick_kernel, out_shape=jax.ShapeDtypeStruct((BLOCK, F), bf...  1.69 us
  transfers between devices with their start and end apart: 1, of which 0 were waited for; matrix products, arithmetic and copies ran while one was open for 0% of the time, Pallas kernels for 0%

profile of v3, /device:TPU:25, one launch (start us, length us, event | category | flops | bytes accessed | tf_op | source)
XLA Modules:
  0.0 34.1 jit_solution(12000693029643128185)
XLA Ops:
  0.0 1.7 %pick_controls.1 = bf16[96,512]{1,0:T(8,128)(2,1)S(1)} custom-call(bf16[1024,512]{1,0:T(8,128)(2,1)} %cells_ref.1, s32[8,128]{1,0:T(8,128)} %bitcast.4, s32[8,128]{1,0:T(8,128)} %bitcast.6), custom_call_target="tpu_custom_call" | custom-call | tf_op jit(solution)/shard_map/pick_controls/pallas_call | solution.py:221
  1.7 7.0 %all_gather.9 = bf16[384,512]{1,0:T(8,128)(2,1)S(1)} all-gather(bf16[96,512]{1,0:T(8,128)(2,1)S(1)} %pick_controls.1), channel_id=1, replica_groups={{0,1,2,3},{4,5,6,7},{8,9,10,11},{12,13,14,15},{16,17,18,19},{20,21,22,2..., dimensions={0}, use_global_device_ids=true | all-gather | bytes 491520 | tf_op jit(solution)/shard_map/all_gather | solution.py:237
  8.7 0.7 %collective-permute-start = (bf16[96,512]{1,0:T(8,128)(2,1)S(1)}, bf16[96,512]{1,0:T(8,128)(2,1)S(1)}, u32[]{:S(2)}, u32[]{:S(2)}) collective-permute-start(bf16[96,512]{1,0:T(8,128)(2,1)S(1)} %slice.4.group_ref), channel_id=1, source_target_pairs={{0,5},{2,7}} | collective-permute-start | bytes 294920 | tf_op jit(solution)/shard_map/ppermute | solution.py:242
  9.4 9.7 %all_gather.10.rows_ref = bf16[576,512]{1,0:T(8,128)(2,1)S(1)} all-gather(bf16[288,512]{1,0:T(8,128)(2,1)S(1)} %constant_dynamic-slice_fusion), channel_id=1, replica_groups={{3,5},{6,8},{11,13},{14,16},{19,21},{22,24},{27,29},{30,32},{35,37},{38..., dimensions={0}, use_global_device_ids=true | all-gather | bytes 884736 | tf_op jit(solution)/shard_map/all_gather | solution.py:243
  19.1 0.0 copy-start
  19.1 0.0 collective-permute-done.first_ref
  19.1 3.8 %sphere.1 = bf16[400,512]{1,0:T(8,128)(2,1)S(1)} custom-call(bf16[576,512]{1,0:T(8,128)(2,1)S(1)} %all_gather.10.rows_ref, bf16[96,512]{1,0:T(8,128)(2,1)S(1)} %slice.4.group_ref, bf16[96,512]{1,0:T(8,128)(2,1)S(1)} %collective-permute-done.first_ref), custom_call_target="tpu_custom_call" | custom-call | tf_op jit(solution)/shard_map/sphere/pallas_call | solution.py:244
  22.9 0.0 copy-start.1
  22.9 9.4 %all_gather.11 = bf16[800,512]{1,0:T(8,128)(2,1)S(1)} all-gather(bf16[400,512]{1,0:T(8,128)(2,1)S(1)} %sphere.1), channel_id=1, replica_groups={{0,1},{2,3},{4,5},{6,7},{8,9},{10,11},{12,13},{14,15},{16,17},{18,19},{..., dimensions={0}, use_global_device_ids=true | all-gather | bytes 1228800 | tf_op jit(solution)/shard_map/all_gather | solution.py:253
  32.3 0.0 copy-done
  32.3 0.0 copy-done.1
  32.3 1.8 %apply_spheres.1 = bf16[1024,512]{1,0:T(8,128)(2,1)} custom-call(bf16[1024,512]{1,0:T(8,128)(2,1)S(1)} %copy-done, s32[8,128]{1,0:T(8,128)S(1)} %bitcast.5, bf16[2,400,512]{2,1,0:T(8,128)(2,1)S(1)} %bitcast.3), custom_call_target="tpu_custom_call" | custom-call | tf_op jit(solution)/shard_map/apply_spheres/pallas_call | solution.py:254
  (2 shorter events, 0.0 us)
Async XLA Ops:
  8.7 10.4 %collective-permute-start = (bf16[96,512]{1,0:T(8,128)(2,1)S(1)}, bf16[96,512]{1,0:T(8,128)(2,1)S(1)}, u32[]{:S(2)}, u32[]{:S(2)}) collective-permute-start(bf16[96,512]{1,0:T(8,128)(2,1)S(1)} %slice.4.group_ref), channel_id=1, source_target_pairs={{0,5},{2,7}} | collective-permute-start | bytes 294920 | tf_op jit(solution)/shard_map/ppermute | solution.py:242
  19.1 13.3 %copy-start = (bf16[1024,512]{1,0:T(8,128)(2,1)S(1)}, bf16[1024,512]{1,0:T(8,128)(2,1)}, u32[]{:S(2)}) copy-start(bf16[1024,512]{1,0:T(8,128)(2,1)} %cells_ref.1) | copy-start | bytes 3145732
  22.9 9.4 %copy-start.1 = (s32[1024]{0:T(1024)S(1)}, s32[1024]{0:T(1024)}, u32[]{:S(2)}) copy-start(s32[1024]{0:T(1024)} %param.4) | copy-start | bytes 12292

commit v4 on v3

--- a/solution.py
+++ b/solution.py
@@ -13,7 +13,7 @@
 LANES = 128
 SUBROWS = ROWS // LANES
 MEMBERS = 4
-CHUNKS = 4
+CHUNKS = 8
 HOME = 3 * BLOCK
 GROUPS = 128
 HALF = F // 2
@@ -36,7 +36,7 @@
 
 
 def pick_kernel(cells_hbm, plate_hbm, control_hbm, out_ref, cells, plate_ref, control_ref, sems, flag_sems):
-    chunk = ROWS // 4
+    chunk = ROWS // 2
     flag_copies = [
         pltpu.make_async_copy(control_hbm, control_ref, flag_sems.at[0]),
         pltpu.make_async_copy(plate_hbm, plate_ref, flag_sems.at[1]),
@@ -45,7 +45,7 @@
         pltpu.make_async_copy(
             cells_hbm.at[pl.ds(part * chunk, chunk)], cells.at[pl.ds(part * chunk, chunk)], sems.at[part]
         )
-        for part in range(4)
+        for part in range(2)
     ]
     for copy in flag_copies + copies:
         copy.start()
@@ -83,7 +83,7 @@
     out_ref[...] = jnp.where(last, jnp.broadcast_to(earlier, (BLOCK, F)), picked).astype(bf16)
 
 
-def sphere_kernel(rows_ref, group_ref, first_ref, out_ref, start_ref, rest_ref, start_b, rest_b, left_b, iterate_b):
+def sphere_kernel(rows_ref, group_ref, first_ref, out_ref, start_ref, rest_ref, raw_b, start_b, rest_b, left_b, iterate_b):
     index = lax.axis_index("d")
     group = index // MEMBERS
     home = (group + index) % 2
@@ -119,6 +119,7 @@
     for part in parts:
         covariance = matmul_tn(picked[:, part], picked) * scale - centre_column[part, :] * centre_row
         start_ref[part, :] = covariance
+        raw_b[part, :] = covariance.astype(bf16)
         squares = squares + jnp.sum(covariance * covariance, axis=0, keepdims=True)
     traces = jnp.zeros((1, LANES), f32)
     for span in quarters:
@@ -130,20 +131,25 @@
         keep_part * keep_part * jnp.sum(squares, keepdims=True) + 2.0 * keep_part * ridge * trace + F * ridge * ridge
     )
     norm_scale = jnp.sqrt(norm_square)
-    inverse_norm = 1.0 / norm_scale
+    slope = keep_part / norm_scale
+    level = ridge / norm_scale
     for part in parts:
-        start_ref[part, :] = start_ref[part, :] * (keep_part * inverse_norm)
-    for span in quarters:
-        start_ref[span, span] = start_ref[span, span] + jnp.where(eye, ridge * inverse_norm, 0.0)
-    for part in parts:
-        start_b[part, :] = start_ref[part, :].astype(bf16)
-    for part in parts:
-        a = start_ref[part, :]
-        square = matmul(start_b[part, :], start_b[...])
-        iterate = 1.5 * a - 0.5 * square
-        left_b[part, :] = (0.25 * square - 1.5 * a).astype(bf16)
-        iterate_b[part, :] = iterate.astype(bf16)
-        rest_ref[part, :] = -0.75 * a - 1.125 * iterate
+        products = matmul(raw_b[part, :], raw_b[...])
+        for row in range(0, HALF, LANES):
+            rows = slice(part.start + row, part.start + row + LANES)
+            for columns in quarters:
+                raw = start_ref[rows, columns]
+                a = slope * raw
+                square = (slope * slope) * products[row : row + LANES, columns] + (2.0 * slope * level) * raw
+                if rows == columns:
+                    a = a + jnp.where(eye, level, 0.0)
+                    square = square + jnp.where(eye, level * level, 0.0)
+                iterate = 1.5 * a - 0.5 * square
+                start_ref[rows, columns] = a
+                start_b[rows, columns] = a.astype(bf16)
+                left_b[rows, columns] = (0.25 * square - 1.5 * a).astype(bf16)
+                iterate_b[rows, columns] = iterate.astype(bf16)
+                rest_ref[rows, columns] = -0.75 * a - 1.125 * iterate
     z = 2.25
     for step in range(2):
         for part in parts:
@@ -227,7 +233,7 @@
             pltpu.VMEM((ROWS, F), bf16),
             pltpu.VMEM((SUBROWS, LANES), jnp.int32),
             pltpu.VMEM((SUBROWS, LANES), jnp.int32),
-            pltpu.SemaphoreType.DMA((4,)),
+            pltpu.SemaphoreType.DMA((2,)),
             pltpu.SemaphoreType.DMA((2,)),
         ],
         compiler_params=params,
@@ -246,7 +252,7 @@
         out_shape=jax.ShapeDtypeStruct((PACK, F), bf16),
         in_specs=[vmem, vmem, vmem],
         out_specs=vmem,
-        scratch_shapes=[pltpu.VMEM((F, F), f32)] * 2 + [pltpu.VMEM((F, F), bf16)] * 4,
+        scratch_shapes=[pltpu.VMEM((F, F), f32)] * 2 + [pltpu.VMEM((F, F), bf16)] * 5,
         compiler_params=params,
         name="sphere",
     )(plate_rows, opening, first)

time: 34.3 us -> 34.1 us (level)
  no operation moved by 1% of the time
where the time goes in v4:
time: 34.1 us; the launch traced here: 33.9 us
  blocking collectives  26.1 us (77%)
  Pallas kernels  7.05 us (21%)
  starting transfers between devices  0.67 us (2%)
    all_gather x1, blocking collectives, shards(): lax.all_gather(side, 'd', axis_index_groups=pairs('plate'), tiled=True)  9.67 us
    all_gather x1, blocking collectives, shards(): lax.all_gather(sphere, 'd', axis_index_groups=pairs('chip'), tiled=True)  9.42 us
    all_gather x1, blocking collectives, shards(): lax.all_gather(block, 'd', axis_index_groups=members, tiled=True)  6.97 us
    pallas_call x1, Pallas kernels, shards(): pl.pallas_call(sphere_kernel, out_shape=jax.ShapeDtypeStruct((PACK, F), b...  3.74 us
    pallas_call x1, Pallas kernels, shards(): pl.pallas_call(apply_kernel, out_shape=jax.ShapeDtypeStruct((ROWS, F), bf...  1.72 us
    pallas_call x1, Pallas kernels, shards(): pl.pallas_call(pick_kernel, out_shape=jax.ShapeDtypeStruct((BLOCK, F), bf...  1.59 us
  transfers between devices with their start and end apart: 1, of which 0 were waited for; matrix products, arithmetic and copies ran while one was open for 0% of the time, Pallas kernels for 0%

profile of v4, /device:TPU:25, one launch (start us, length us, event | category | flops | bytes accessed | tf_op | source)
XLA Modules:
  0.0 33.9 jit_solution(1806059192117243178)
XLA Ops:
  0.0 1.6 %pick_controls.1 = bf16[96,512]{1,0:T(8,128)(2,1)S(1)} custom-call(bf16[1024,512]{1,0:T(8,128)(2,1)} %cells_ref.1, s32[8,128]{1,0:T(8,128)} %bitcast.4, s32[8,128]{1,0:T(8,128)} %bitcast.6), custom_call_target="tpu_custom_call" | custom-call | tf_op jit(solution)/shard_map/pick_controls/pallas_call | solution.py:227
  1.6 7.0 %all_gather.9 = bf16[384,512]{1,0:T(8,128)(2,1)S(1)} all-gather(bf16[96,512]{1,0:T(8,128)(2,1)S(1)} %pick_controls.1), channel_id=1, replica_groups={{0,1,2,3},{4,5,6,7},{8,9,10,11},{12,13,14,15},{16,17,18,19},{20,21,22,2..., dimensions={0}, use_global_device_ids=true | all-gather | bytes 491520 | tf_op jit(solution)/shard_map/all_gather | solution.py:243
  8.6 0.7 %collective-permute-start = (bf16[96,512]{1,0:T(8,128)(2,1)S(1)}, bf16[96,512]{1,0:T(8,128)(2,1)S(1)}, u32[]{:S(2)}, u32[]{:S(2)}) collective-permute-start(bf16[96,512]{1,0:T(8,128)(2,1)S(1)} %slice.4.group_ref), channel_id=1, source_target_pairs={{0,5},{2,7}} | collective-permute-start | bytes 294920 | tf_op jit(solution)/shard_map/ppermute | solution.py:248
  9.3 9.7 %all_gather.10.rows_ref = bf16[576,512]{1,0:T(8,128)(2,1)S(1)} all-gather(bf16[288,512]{1,0:T(8,128)(2,1)S(1)} %constant_dynamic-slice_fusion), channel_id=1, replica_groups={{3,5},{6,8},{11,13},{14,16},{19,21},{22,24},{27,29},{30,32},{35,37},{38..., dimensions={0}, use_global_device_ids=true | all-gather | bytes 884736 | tf_op jit(solution)/shard_map/all_gather | solution.py:249
  19.0 0.0 copy-start
  19.0 0.0 collective-permute-done.first_ref
  19.0 3.7 %sphere.1 = bf16[400,512]{1,0:T(8,128)(2,1)S(1)} custom-call(bf16[576,512]{1,0:T(8,128)(2,1)S(1)} %all_gather.10.rows_ref, bf16[96,512]{1,0:T(8,128)(2,1)S(1)} %slice.4.group_ref, bf16[96,512]{1,0:T(8,128)(2,1)S(1)} %collective-permute-done.first_ref), custom_call_target="tpu_custom_call" | custom-call | tf_op jit(solution)/shard_map/sphere/pallas_call | solution.py:250
  22.7 0.0 copy-start.1
  22.7 9.4 %all_gather.11 = bf16[800,512]{1,0:T(8,128)(2,1)S(1)} all-gather(bf16[400,512]{1,0:T(8,128)(2,1)S(1)} %sphere.1), channel_id=1, replica_groups={{0,1},{2,3},{4,5},{6,7},{8,9},{10,11},{12,13},{14,15},{16,17},{18,19},{..., dimensions={0}, use_global_device_ids=true | all-gather | bytes 1228800 | tf_op jit(solution)/shard_map/all_gather | solution.py:259
  32.2 0.0 copy-done
  32.2 0.0 copy-done.1
  32.2 1.7 %apply_spheres.1 = bf16[1024,512]{1,0:T(8,128)(2,1)} custom-call(bf16[1024,512]{1,0:T(8,128)(2,1)S(1)} %copy-done, s32[8,128]{1,0:T(8,128)S(1)} %bitcast.5, bf16[2,400,512]{2,1,0:T(8,128)(2,1)S(1)} %bitcast.3), custom_call_target="tpu_custom_call" | custom-call | tf_op jit(solution)/shard_map/apply_spheres/pallas_call | solution.py:260
  (2 shorter events, 0.0 us)
Async XLA Ops:
  8.6 10.4 %collective-permute-start = (bf16[96,512]{1,0:T(8,128)(2,1)S(1)}, bf16[96,512]{1,0:T(8,128)(2,1)S(1)}, u32[]{:S(2)}, u32[]{:S(2)}) collective-permute-start(bf16[96,512]{1,0:T(8,128)(2,1)S(1)} %slice.4.group_ref), channel_id=1, source_target_pairs={{0,5},{2,7}} | collective-permute-start | bytes 294920 | tf_op jit(solution)/shard_map/ppermute | solution.py:248
  19.0 13.2 %copy-start = (bf16[1024,512]{1,0:T(8,128)(2,1)S(1)}, bf16[1024,512]{1,0:T(8,128)(2,1)}, u32[]{:S(2)}) copy-start(bf16[1024,512]{1,0:T(8,128)(2,1)} %cells_ref.1) | copy-start | bytes 3145732
  22.7 9.4 %copy-start.1 = (s32[1024]{0:T(1024)S(1)}, s32[1024]{0:T(1024)}, u32[]{:S(2)}) copy-start(s32[1024]{0:T(1024)} %param.4) | copy-start | bytes 12292

commit v5 on v4

--- a/solution.py
+++ b/solution.py
@@ -86,7 +86,7 @@
 def sphere_kernel(rows_ref, group_ref, first_ref, out_ref, start_ref, rest_ref, raw_b, start_b, rest_b, left_b, iterate_b):
     index = lax.axis_index("d")
     group = index // MEMBERS
-    home = (group + index) % 2
+    home = (index + index // 2) % 2
     last_home = (group == GROUPS - 1) & (home == 1)
     first_plate = group + home == 1
     slot = lax.broadcasted_iota(jnp.int32, (BLOCK, LANES), 0).astype(f32)
@@ -179,7 +179,7 @@
 
 def apply_kernel(cells_ref, plate_ref, packed_ref, out_hbm, out, spheres, sems):
     group = lax.axis_index("d") // MEMBERS
-    parity = group % 2
+    parity = lax.axis_index("d") // 2 % 2
     earlier = jnp.sum(jnp.where(plate_ref[...] < group, 1, 0))
     offsets = []
     for side, core in enumerate((parity, 1 - parity)):
@@ -213,10 +213,9 @@
 def pairs(kind):
     if kind == "chip":
         return [[2 * i, 2 * i + 1] for i in range(GROUPS * MEMBERS // 2)]
-    first = [MEMBERS * p + 1 - p % 2 for p in range(GROUPS)]
-    near = [[d + 2, d + 4] for d in first[:-1]]
-    far = [[d, d + 6] for d in first[:-1]]
-    return near + far + [[0, 2], [first[-1], first[-1] + 2]]
+    near = [[4 * p + 2, 4 * p + 4] for p in range(GROUPS - 1)]
+    far = [[4 * p + 1, 4 * p + 7] for p in range(GROUPS - 1)]
+    return near + far + [[0, 3], [4 * GROUPS - 3, 4 * GROUPS - 2]]
 
 
 def shards(cells, plate_id, control):
@@ -242,10 +241,10 @@
     members = [[MEMBERS * g + m for m in range(MEMBERS)] for g in range(GROUPS)]
     group_rows = lax.all_gather(block, "d", axis_index_groups=members, tiled=True)
     index = lax.axis_index("d")
-    home = (index ^ (index >> 2)) & 1
+    home = (index ^ (index >> 1)) & 1
     side = lax.dynamic_slice_in_dim(group_rows, home * BLOCK, HOME, 0)
     opening = group_rows[0:BLOCK]
-    first = lax.ppermute(opening, "d", [(0, 5), (2, 7)])
+    first = lax.ppermute(opening, "d", [(0, 4), (2, 7)])
     plate_rows = lax.all_gather(side, "d", axis_index_groups=pairs("plate"), tiled=True)
     sphere = pl.pallas_call(
         sphere_kernel,

time: 34.1 us -> 34.1 us (level)
  no operation moved by 1% of the time
where the time goes in v5:
time: 34.1 us; the launch traced here: 33.9 us
  blocking collectives  26.1 us (77%)
  Pallas kernels  7.05 us (21%)
  starting transfers between devices  0.67 us (2%)
    all_gather x1, blocking collectives, shards(): lax.all_gather(side, 'd', axis_index_groups=pairs('plate'), tiled=True)  9.67 us
    all_gather x1, blocking collectives, shards(): lax.all_gather(sphere, 'd', axis_index_groups=pairs('chip'), tiled=True)  9.44 us
    all_gather x1, blocking collectives, shards(): lax.all_gather(block, 'd', axis_index_groups=members, tiled=True)  6.97 us
    pallas_call x1, Pallas kernels, shards(): pl.pallas_call(sphere_kernel, out_shape=jax.ShapeDtypeStruct((PACK, F), b...  3.74 us
    pallas_call x1, Pallas kernels, shards(): pl.pallas_call(apply_kernel, out_shape=jax.ShapeDtypeStruct((ROWS, F), bf...  1.72 us
    pallas_call x1, Pallas kernels, shards(): pl.pallas_call(pick_kernel, out_shape=jax.ShapeDtypeStruct((BLOCK, F), bf...  1.59 us
  transfers between devices with their start and end apart: 1, of which 0 were waited for; matrix products, arithmetic and copies ran while one was open for 0% of the time, Pallas kernels for 0%

profile of v5, /device:TPU:25, one launch (start us, length us, event | category | flops | bytes accessed | tf_op | source)
XLA Modules:
  0.0 33.9 jit_solution(12233671261808535132)
XLA Ops:
  0.0 1.6 %pick_controls.1 = bf16[96,512]{1,0:T(8,128)(2,1)S(1)} custom-call(bf16[1024,512]{1,0:T(8,128)(2,1)} %cells_ref.1, s32[8,128]{1,0:T(8,128)} %bitcast.4, s32[8,128]{1,0:T(8,128)} %bitcast.6), custom_call_target="tpu_custom_call" | custom-call | tf_op jit(solution)/shard_map/pick_controls/pallas_call | solution.py:226
  1.6 7.0 %all_gather.9 = bf16[384,512]{1,0:T(8,128)(2,1)S(1)} all-gather(bf16[96,512]{1,0:T(8,128)(2,1)S(1)} %pick_controls.1), channel_id=1, replica_groups={{0,1,2,3},{4,5,6,7},{8,9,10,11},{12,13,14,15},{16,17,18,19},{20,21,22,2..., dimensions={0}, use_global_device_ids=true | all-gather | bytes 491520 | tf_op jit(solution)/shard_map/all_gather | solution.py:242
  8.6 0.7 %collective-permute-start = (bf16[96,512]{1,0:T(8,128)(2,1)S(1)}, bf16[96,512]{1,0:T(8,128)(2,1)S(1)}, u32[]{:S(2)}, u32[]{:S(2)}) collective-permute-start(bf16[96,512]{1,0:T(8,128)(2,1)S(1)} %slice.4.group_ref), channel_id=1, source_target_pairs={{0,4},{2,7}} | collective-permute-start | bytes 294920 | tf_op jit(solution)/shard_map/ppermute | solution.py:247
  9.3 9.7 %all_gather.10.rows_ref = bf16[576,512]{1,0:T(8,128)(2,1)S(1)} all-gather(bf16[288,512]{1,0:T(8,128)(2,1)S(1)} %constant_dynamic-slice_fusion), channel_id=1, replica_groups={{2,4},{6,8},{10,12},{14,16},{18,20},{22,24},{26,28},{30,32},{34,36},{38..., dimensions={0}, use_global_device_ids=true | all-gather | bytes 884736 | tf_op jit(solution)/shard_map/all_gather | solution.py:248
  19.0 0.0 copy-start
  19.0 0.0 collective-permute-done.first_ref
  19.0 3.7 %sphere.1 = bf16[400,512]{1,0:T(8,128)(2,1)S(1)} custom-call(bf16[576,512]{1,0:T(8,128)(2,1)S(1)} %all_gather.10.rows_ref, bf16[96,512]{1,0:T(8,128)(2,1)S(1)} %slice.4.group_ref, bf16[96,512]{1,0:T(8,128)(2,1)S(1)} %collective-permute-done.first_ref), custom_call_target="tpu_custom_call" | custom-call | tf_op jit(solution)/shard_map/sphere/pallas_call | solution.py:249
  22.7 0.0 copy-start.1
  22.7 9.4 %all_gather.11 = bf16[800,512]{1,0:T(8,128)(2,1)S(1)} all-gather(bf16[400,512]{1,0:T(8,128)(2,1)S(1)} %sphere.1), channel_id=1, replica_groups={{0,1},{2,3},{4,5},{6,7},{8,9},{10,11},{12,13},{14,15},{16,17},{18,19},{..., dimensions={0}, use_global_device_ids=true | all-gather | bytes 1228800 | tf_op jit(solution)/shard_map/all_gather | solution.py:258
  32.2 0.0 copy-done
  32.2 0.0 copy-done.1
  32.2 1.7 %apply_spheres.1 = bf16[1024,512]{1,0:T(8,128)(2,1)} custom-call(bf16[1024,512]{1,0:T(8,128)(2,1)S(1)} %copy-done, s32[8,128]{1,0:T(8,128)S(1)} %bitcast.5, bf16[2,400,512]{2,1,0:T(8,128)(2,1)S(1)} %bitcast.3), custom_call_target="tpu_custom_call" | custom-call | tf_op jit(solution)/shard_map/apply_spheres/pallas_call | solution.py:259
  (2 shorter events, 0.0 us)
Async XLA Ops:
  8.6 10.4 %collective-permute-start = (bf16[96,512]{1,0:T(8,128)(2,1)S(1)}, bf16[96,512]{1,0:T(8,128)(2,1)S(1)}, u32[]{:S(2)}, u32[]{:S(2)}) collective-permute-start(bf16[96,512]{1,0:T(8,128)(2,1)S(1)} %slice.4.group_ref), channel_id=1, source_target_pairs={{0,4},{2,7}} | collective-permute-start | bytes 294920 | tf_op jit(solution)/shard_map/ppermute | solution.py:247
  19.0 13.2 %copy-start = (bf16[1024,512]{1,0:T(8,128)(2,1)S(1)}, bf16[1024,512]{1,0:T(8,128)(2,1)}, u32[]{:S(2)}) copy-start(bf16[1024,512]{1,0:T(8,128)(2,1)} %cells_ref.1) | copy-start | bytes 3145732
  22.7 9.5 %copy-start.1 = (s32[1024]{0:T(1024)S(1)}, s32[1024]{0:T(1024)}, u32[]{:S(2)}) copy-start(s32[1024]{0:T(1024)} %param.4) | copy-start | bytes 12292
